TPU v7x, 256 devices: a whole 4x4x8 slice. The times are simulated.
256 devices in a mesh: dp: 4 (over x), mp: 64 (over y, z, core).
Axes of the slice: x: 4, y: 4, z: 8, core: 2. Of those that a mesh axis runs over, the one named last changes fastest.
Arguments:
- tokens: bfloat16 [1024, 8192], P('dp', 'mp'), may hold values from -6 to 6
- gate_act: bfloat16 [1024, 16384], P('dp', 'mp'), may hold values from -6 to 6
- up_act: bfloat16 [1024, 16384], P('dp', 'mp'), may hold values from -6 to 6
- hidden_grad: bfloat16 [1024, 16384], P('dp', 'mp'), may hold values from -0.59765625 to 0.59765625
- gate_weight: bfloat16 [8192, 16384], P(None, 'mp'), may hold values from -0.375 to 0.375
- up_weight: bfloat16 [8192, 16384], P(None, 'mp'), may hold values from -0.375 to 0.375
- block_mask: int32 [2, 64, 128], replicated, may hold values from 0 to 1, as said below
- row_perm: int32 [2, 64], replicated, may hold values from 0 to 63, as said below
- scale_exp: int32 [2, 64, 128], replicated, may hold values from 1 to 2
Outputs:
- input_grad: bfloat16 [1024, 8192], P('dp', 'mp')
- weight_grads: float32 [2, 8192, 16384], P(None, ('mp', 'dp'))
Inputs may be any that keep to these rules, and one draw needn't show every extreme that they name: `block_mask`: within a row block, each of the 64 column groups of 2 block columns holds the same number of kept blocks, at most 1; positions k of row_perm from o * 1 to (o + 1) - 1 belong to owner o, and for each matrix all row blocks of some owner hold exactly 1 kept blocks in every column group. `row_perm`: for each matrix a permutation of the row blocks.
All inputs are finite; a program needn't handle non-finite values.
Results may differ from a plain program's by a relative error of at most 0.012.
Values may be sent and summed in bfloat16 or wider, within the bound.
A program may use at most 128 MiB of HBM per device.

v0:
```python
import jax
import jax.numpy as jnp
from jax import lax
from jax.sharding import PartitionSpec as P

BLOCK = 128


def body(
    tokens, gate_act, up_act, hidden_grad, gate_weight, up_weight, block_mask, row_perm, scale_exp
):
    groups = lax.axis_size("mp")
    quarters = lax.axis_size("dp")
    member = lax.axis_index("mp")
    quarter = lax.axis_index("dp")
    width = gate_act.shape[1]
    col_blocks = width // BLOCK
    rows_total = gate_weight.shape[0]
    row_blocks = rows_total // BLOCK
    own_rows = row_blocks // groups
    unit_rows = BLOCK // quarters
    qlen = own_rows * unit_rows
    gate_f = gate_act.astype(jnp.float32)
    sig = jax.nn.sigmoid(gate_f)
    hid_f = hidden_grad.astype(jnp.float32)
    gate_grad = (hid_f * up_act.astype(jnp.float32) * sig * (1.0 + gate_f * (1.0 - sig))).astype(
        jnp.bfloat16
    )
    up_grad = (hid_f * gate_f * sig).astype(jnp.bfloat16)
    local_mask = lax.dynamic_slice_in_dim(block_mask, member * col_blocks, col_blocks, 2)
    mask_factor = local_mask[:, :, None, :, None]
    stacked = jnp.stack([gate_weight, up_weight]).reshape(2, row_blocks, BLOCK, col_blocks, BLOCK)
    weights = (stacked * mask_factor.astype(jnp.bfloat16)).reshape(2, rows_total, width)
    dims = (((1,), (1,)), ((), ()))
    first = lax.dot_general(weights[0], gate_grad, dims, preferred_element_type=jnp.float32)
    summed_in = lax.psum_scatter(
        first + lax.dot_general(weights[1], up_grad, dims, preferred_element_type=jnp.float32),
        "mp",
        scatter_dimension=0,
        tiled=True,
    )
    input_grad = summed_in.T.astype(jnp.bfloat16)
    both = jnp.concatenate([gate_grad, up_grad], axis=1)
    full_grads = lax.dot_general(
        lax.all_gather(tokens, "mp", axis=1, tiled=True),
        both,
        (((0,), (0,)), ((), ())),
        preferred_element_type=jnp.float32,
    )
    local_exp = lax.dynamic_slice_in_dim(scale_exp, member * col_blocks, col_blocks, 2)
    block_factor = local_mask.astype(jnp.float32) * jnp.exp2(-local_exp.astype(jnp.float32))
    grad_view = jnp.stack([full_grads[:, :width], full_grads[:, width:]]).reshape(
        2, row_blocks, BLOCK, col_blocks, BLOCK
    )
    clipped = jnp.clip(grad_view * block_factor[:, :, None, :, None], -1.0, 1.0).astype(
        jnp.bfloat16
    )
    clipped = clipped.reshape(2, row_blocks, BLOCK, width)
    owned = jnp.take_along_axis(clipped, row_perm[:, :, None, None], axis=1).reshape(
        2, rows_total, width
    )
    positions = (
        member * own_rows * BLOCK + quarter * qlen + jnp.arange(qlen, dtype=jnp.int32)
    ) // BLOCK
    source_rows = jnp.take(row_perm, positions, axis=1)
    row_exp = jnp.take_along_axis(scale_exp, source_rows[:, :, None], axis=1)
    up_scale = jnp.exp2(row_exp.astype(jnp.float32))[:, :, :, None]
    moved = lax.all_to_all(owned, "mp", split_axis=1, concat_axis=2, tiled=True)
    summed = lax.psum_scatter(moved, "dp", scatter_dimension=1, tiled=True).astype(jnp.float32)
    all_cols = summed.shape[2] // BLOCK
    scaled = summed.reshape(2, qlen, all_cols, BLOCK) * up_scale
    return (input_grad, scaled.reshape(2, qlen, all_cols * BLOCK))


def solution(mesh):
    in_specs = (
        P("dp", "mp"),
        P("dp", "mp"),
        P("dp", "mp"),
        P("dp", "mp"),
        P(None, "mp"),
        P(None, "mp"),
        P(),
        P(),
        P(),
    )
    out_specs = (P("dp", "mp"), P(None, ("mp", "dp"), None))
    return jax.shard_map(body, mesh=mesh, in_specs=in_specs, out_specs=out_specs, check_vma=False)
```

profile of v0, /device:TPU:1, one launch (start us, length us, event | category | flops | bytes accessed | tf_op | source)
XLA Modules:
  0.0 638.9 jit_solution(15789610550575422868)
XLA Ops:
  7.2 0.0 all-gather.2.cloned.1.call-start
  7.2 0.7 all-gather.2.cloned.1.call-update
  7.9 1.0 constant_dynamic-slice_fusion
  8.9 0.1 copy.63
  9.0 0.1 copy.64
  9.1 0.1 copy.50
  9.2 0.2 mul.73
  9.4 0.1 mul.74
  9.5 0.7 bitcast_or_fusion
  10.2 0.1 reshape.180
  10.3 0.7 compare_and_fusion.2
  11.0 0.1 copy.46
  11.1 0.1 copy.45
  11.2 0.0 copy-start.2
  11.2 0.0 copy-start.3
  11.2 6.9 %stack.18 = bf16[1,64,128,2,128]{4,3,2,1,0:T(2,128)(2,1)} reshape(bf16[8192,256]{1,0:T(8,128)(2,1)} %param.13) | data formatting | bytes 8388608 | tf_op jit(solution)/shard_map/stack | solution.py:32
  18.2 6.9 %stack.19 = bf16[1,64,128,2,128]{4,3,2,1,0:T(2,128)(2,1)} reshape(bf16[8192,256]{1,0:T(8,128)(2,1)} %param.14) | data formatting | bytes 8388608 | tf_op jit(solution)/shard_map/stack | solution.py:32
  25.1 0.0 copy-done.1
  25.1 0.0 copy-done.2
  25.1 0.0 copy-done.3
  25.1 0.1 fusion.15
  25.2 65.9 %all-gather.2.cloned.1.call-done = bf16[256,8192]{1,0:T(8,128)(2,1)} async-done(((bf16[256,128]{1,0:T(8,128)(2,1)}), bf16[256,8192]{1,0:T(8,128)(2,1)}) %all-gather.2.cloned.1.call-update) | async-done | bytes 4194320 | tf_op jit(solution)/shard_map/all_gather | solution.py:45
  91.1 4.6 convolution_bitcast_fusion
  95.7 6.3 fusion.24
  102.0 9.0 %copy.61 = f32[8192,256]{1,0:T(8,128)} copy(f32[8192,256]{0,1:T(8,128)} %get-tuple-element.12) | data formatting | bytes 16777216 | tf_op jit(solution)/shard_map/stack | solution.py:52
  111.0 9.0 %copy.62 = f32[8192,256]{1,0:T(8,128)} copy(f32[8192,256]{0,1:T(8,128)} %get-tuple-element.13) | data formatting | bytes 16777216 | tf_op jit(solution)/shard_map/stack | solution.py:52
  120.0 9.7 %fusion.1 = bf16[2,64,128,256]{3,2,1,0:T(8,128)(2,1)} fusion(f32[1,64,128,256]{3,2,1,0:T(8,128)} %bitcast.46, f32[1,64,128,256]{3,2,1,0:T(8,128)} %bitcast.45, f32[2,64,256]{2,1,0:T(8,128)S(1)} %mul.74), kind=kLoop, calls=%fused_computation.5 | loop fusion | flops 16777216 | bytes 25296896 | tf_op jit(solution)/shard_map/convert_element_type | solution.py:55
  129.7 10.6 %gather_fusion.1 = bf16[128,128,256]{2,1,0:T(8,128)(2,1)} fusion(bf16[2,64,128,256]{3,2,1,0:T(8,128)(2,1)} %fusion.1, s32[128]{0:T(128)S(1)} %reshape.180), kind=kCustom, calls=%fused_computation.1 | custom fusion | bytes 16778240 | tf_op jit(solution)/shard_map/jit(take_along_axis)/gather | solution.py:59
  140.3 0.3 broadcast_in_dim.39
  140.6 63.5 %broadcast_select_fusion = bf16[2,8192,256]{2,0,1:T(2,128)(2,1)} fusion(pred[2,8192]{0,1:T(8,128)(4,1)S(1)} %bitcast.52, bf16[2,8192,256]{2,1,0:T(8,128)(2,1)} %bitcast.47), kind=kLoop, calls=%fused_computation.6 | loop fusion | flops 4194304 | bytes 16793600 | tf_op jit(solution)/shard_map/jit(take_along_axis)/select_n | solution.py:59
  204.1 8.6 %all-to-all-start = ((bf16[2,8192,256]{2,0,1:T(2,128)(2,1)}), bf16[2,8192,256]{2,0,1:T(2,128)(2,1)}, u32[]{:S(2)}, u32[]{:S(2)}) async-start(bf16[2,8192,256]{2,0,1:T(2,128)(2,1)} %broadcast_select_fusion), calls=%async_computation.1 | async-start | bytes 16777216 | tf_op jit(solution)/shard_map/all_to_all | solution.py:68
  212.6 0.2 reduce-scatter.2.cloned.1.call-start
  212.9 15.6 %maximum_multiply_fusion.1 = bf16[2,64,128,2,128]{4,3,2,1,0:T(2,128)(2,1)S(1)} fusion(bf16[1,64,128,2,128]{4,3,2,1,0:T(2,128)(2,1)} %stack.19, bf16[1,64,128,2,128]{4,3,2,1,0:T(2,128)(2,1)} %stack.18, bf16[2,64,2]{2,1,0:T(8,128)(2,1)S(1)} %copy.45), kind=kLoop, calls=%fused_computation.9 | loop fusion | flops 8388608 | bytes 16777728 | tf_op jit(solution)/shard_map/mul | solution.py:33
  228.5 5.9 fusion.25
  234.4 1.3 fusion.4
  235.7 4.5 convolution_add_fusion
  240.2 0.0 reduce-scatter.2.cloned.1.call-update
  240.2 0.0 all-reduce.3.cloned.1.call-start
  240.3 179.1 %all-to-all-done = bf16[2,8192,256]{2,0,1:T(2,128)(2,1)} async-done(((bf16[2,8192,256]{2,0,1:T(2,128)(2,1)}), bf16[2,8192,256]{2,0,1:T(2,128)(2,1)}, u32[]{:S(2)}, u32[]{:S(2)}) %all-to-all-start) | async-done | bytes 8388640 | tf_op jit(solution)/shard_map/all_to_all | solution.py:68
  419.3 7.7 %copy.52 = bf16[2,8192,256]{2,1,0:T(8,128)(2,1)} copy(bf16[2,8192,256]{2,0,1:T(2,128)(2,1)} %all-to-all-done) | data formatting | bytes 16777216 | tf_op jit(solution)/shard_map/all_to_all | solution.py:68
  427.1 12.0 %copy.53 = bf16[2,128,64,256]{1,3,2,0:T(8,128)(2,1)} copy(bf16[2,128,64,256]{3,1,2,0:T(8,128)(2,1)} %bitcast.48) | data formatting | bytes 16777216 | tf_op jit(solution)/shard_map/all_to_all | solution.py:68
  439.0 21.3 %copy.54 = bf16[2,128,16384]{2,0,1:T(2,128)(2,1)} copy(bf16[2,128,16384]{1,2,0:T(8,128)(2,1)} %bitcast.49) | data formatting | bytes 16777216 | tf_op jit(solution)/shard_map/all_to_all | solution.py:68
  460.4 0.0 all-reduce.3.cloned.1.call-update
  460.4 0.0 copy-start.5
  460.4 0.6 copy-done.4
  461.1 0.1 copy.55
  461.2 0.6 gather_fusion
  461.8 0.1 copy.57
  461.9 0.1 reshape.186
  461.9 0.0 copy-done
  462.0 0.9 gather_fusion.2
  462.8 0.1 compare_and_fusion
  462.9 0.1 copy.56
  463.0 0.1 multiply_exponential_fusion
  463.1 2.6 mul.79
  465.8 6.2 mul.80
  472.0 0.0 copy-done.5
  472.0 0.6 dynamic-slice
  473.2 0.0 reduce-scatter.2.cloned.1.call-done
  473.2 0.9 convert_bitcast_fusion
  474.1 0.7 copy.59
  474.9 147.9 %all-reduce.3.cloned.1.call-done = bf16[2,128,16384]{2,0,1:T(2,128)(2,1)} async-done(((bf16[2,128,16384]{2,0,1:T(2,128)(2,1)}), bf16[2,128,16384]{2,0,1:T(2,128)(2,1)}) %all-reduce.3.cloned.1.call-update) | async-done | bytes 8388624
  622.7 5.2 convert_multiply_fusion
  627.9 4.4 copy.60
  (10 shorter events, 0.1 us)
Async XLA Ops:
  7.2 84.0 %all-gather.2.cloned.1.call-start = ((), (), s32[]{:S(2)}) async-start(), calls=%async_computation.3 | async-start | bytes 4259840 | tf_op jit(solution)/shard_map/all_gather | solution.py:45
  11.2 13.9 %copy-start.1 = (bf16[256,256]{1,0:T(8,128)(2,1)S(1)}, bf16[256,256]{1,0:T(8,128)(2,1)}, u32[]{:S(2)}) copy-start(bf16[256,256]{1,0:T(8,128)(2,1)} %param.10) | copy-start | bytes 393220
  11.2 13.9 %copy-start.2 = (bf16[256,256]{1,0:T(8,128)(2,1)S(1)}, bf16[256,256]{1,0:T(8,128)(2,1)}, u32[]{:S(2)}) copy-start(bf16[256,256]{1,0:T(8,128)(2,1)} %param.12) | copy-start | bytes 393220
  11.2 13.9 %copy-start.3 = (bf16[256,256]{1,0:T(8,128)(2,1)S(1)}, bf16[256,256]{1,0:T(8,128)(2,1)}, u32[]{:S(2)}) copy-start(bf16[256,256]{1,0:T(8,128)(2,1)} %param.11) | copy-start | bytes 393220
  204.1 215.3 %all-to-all-start = ((bf16[2,8192,256]{2,0,1:T(2,128)(2,1)}), bf16[2,8192,256]{2,0,1:T(2,128)(2,1)}, u32[]{:S(2)}, u32[]{:S(2)}) async-start(bf16[2,8192,256]{2,0,1:T(2,128)(2,1)} %broadcast_select_fusion), calls=%async_computation.1 | async-start | bytes 16777216 | tf_op jit(solution)/shard_map/all_to_all | solution.py:68
  212.6 260.6 %reduce-scatter.2.cloned.1.call-start = ((), (), s32[]{:S(2)}) async-start(), calls=%async_computation.2 | async-start | bytes 8519680 | tf_op jit(solution)/shard_map/reduce_scatter | solution.py:36
  240.2 382.5 %all-reduce.3.cloned.1.call-start = ((), (), s32[]{:S(2)}) async-start(), calls=%async_computation.4 | async-start | bytes 16777216
  460.4 0.7 copy-start.4
  460.4 1.6 copy-start
  460.4 11.6 %copy-start.5 = (u32[256]{0:T(256)S(1)}, u32[256]{0:T(256)}, u32[]{:S(2)}) copy-start(u32[256]{0:T(256)} %constant.105) | copy-start | bytes 3076
Sparse Core Ops, SparseCore 0:
  10.5 80.5 all-gather.1
  240.4 191.3 reduce-scatter.1
  460.5 162.1 all-reduce.2
where the time goes:
time: 641 us; the launch traced here: 639 us
  waiting for transfers between devices  394 us (61%)
  local copies, waits for them, and re-layouts  115 us (18%)
  other arithmetic  96.7 us (15%)
  between operations  14.6 us (2%)
  matrix products  10.4 us (2%)
  starting transfers between devices  8.86 us (1%)
    all_to_all x1, waiting for transfers between devices, body(): moved = lax.all_to_all(owned, 'mp', split_axis=1, concat_axis=2, tiled=True)  179 us
    unnamed x4, waiting for transfers between devices  149 us
    all_gather x1, waiting for transfers between devices, body(): lax.all_gather(tokens, 'mp', axis=1, tiled=True)  65.9 us
    select_n x1, other arithmetic, body(): jnp.take_along_axis(clipped, row_perm[:, :, None, None], axis=1)  63.5 us
    all_to_all x3, local copies, waits for them, and re-layouts, body(): moved = lax.all_to_all(owned, 'mp', split_axis=1, concat_axis=2, tiled=True)  41 us
    another operation x2, local copies, waits for them, and re-layouts, body(): jnp.stack([full_grads[:, :width], full_grads[:, width:]])  18 us
    mul x1, other arithmetic, body(): stacked * mask_factor.astype(jnp.bfloat16)  15.6 us
    another operation x2, local copies, waits for them, and re-layouts, body(): jnp.stack([gate_weight, up_weight])  13.8 us
  transfers between devices with their start and end apart: 4, of which 3 were waited for; matrix products, arithmetic and copies ran while one was open for 15% of the time, Pallas kernels for 0%

commit v1 on v0

v1 whole, which is shorter than its diff:
```python
import functools

import jax
import jax.numpy as jnp
from jax import lax
from jax.experimental import pallas as pl
from jax.experimental.pallas import tpu as pltpu
from jax.sharding import PartitionSpec as P

BF = jnp.bfloat16
F32 = jnp.float32
MESH = pl.DeviceIdType.MESH
NX, NY, NZ, NC = 4, 4, 8, 2
NM = NY * NZ * NC
HALF = 16
N_SEM = 96


def slot_of(o):
    return jnp.where(o <= 3, 2 * o, jnp.where(o == 4, 7, 2 * (8 - o) - 1))


def static_slot(o):
    o %= 8
    return 2 * o if o <= 3 else (7 if o == 4 else 2 * (8 - o) - 1)


def kernel(
    tok_ref, g_ref, u_ref, h_ref, wg_ref, wu_ref, mask_ref, perm_ref, exp_ref,
    ig_ref, recv_ref, fac_ref,
    tok, gact, uact, hgrad, wg, wu, xsrc, tt0, tt1, G, GT, wm, facx, lhs, fs, abuf,
    part, crecv, ysum, yrA, yrB, yr2m, yr2p, zr,
    ss, rs, a_ss, a_rs, lsem,
):
    q = lax.axis_index("dp")
    m = lax.axis_index("mp")
    c = lax.rem(m, NC)
    z = lax.rem(lax.div(m, NC), NZ)
    y = lax.div(m, NC * NZ)
    yp, ym, yo = lax.rem(y + 1, NY), lax.rem(y + 3, NY), lax.rem(y + 2, NY)

    def mp_of(yy, zz, cc):
        return (yy * NZ + zz) * NC + cc

    dev_yp, dev_ym = (q, mp_of(yp, z, c)), (q, mp_of(ym, z, c))
    dev_sib = (q, mp_of(y, z, 1 - c))

    def dev_z(d):
        return (q, mp_of(y, lax.rem(z + d, NZ), c))

    def dev_x(d):
        return (lax.rem(q + d, NX), m)

    tts = (tt0, tt1)

    loads = []
    for i, (src, dst) in enumerate(
        ((tok_ref, tok), (g_ref, gact), (u_ref, uact), (h_ref, hgrad))
    ):
        cp = pltpu.make_async_copy(src, dst, lsem.at[i])
        cp.start()
        loads.append(cp)
    wloads = []
    for i, (src, dst) in enumerate(((wg_ref, wg), (wu_ref, wu))):
        cp = pltpu.make_async_copy(src, dst, lsem.at[4 + i])
        cp.start()
        wloads.append(cp)

    barrier = pltpu.get_barrier_semaphore()

    def greet(i, carry):
        pl.semaphore_signal(
            barrier, inc=1, device_id=(q, lax.rem(m + i, NM)), device_id_type=MESH
        )
        return carry

    lax.fori_loop(1, NM, greet, 0)
    for d in range(1, NX):
        pl.semaphore_signal(barrier, inc=1, device_id=dev_x(d), device_id_type=MESH)

    loads[0].wait()
    tok_t = tok[...].T
    for h in range(2):
        for k in range(NX):
            xsrc[h, k] = tok_t[32 * k + HALF * h : 32 * k + HALF * (h + 1), :]
        tts[h][c, y, 0, q] = xsrc[h, q]

    pl.semaphore_wait(barrier, NM - 1 + NX - 1)

    sent = []

    def send(src, dst, dev):
        i = len(sent)
        cp = pltpu.make_async_remote_copy(
            src_ref=src, dst_ref=dst, send_sem=ss.at[i], recv_sem=rs.at[i],
            device_id=dev, device_id_type=MESH,
        )
        cp.start()
        sent.append(cp)
        return cp

    xcp = [[], []]
    for h in range(2):
        for d in (1, 3, 2):
            to = lax.rem(q + d, NX)
            xcp[h].append(send(xsrc.at[h, to], tts[h].at[c, y, 0, q], dev_x(d)))

    for cp in loads[1:]:
        cp.wait()
    gf = gact[...].astype(F32)
    hf = hgrad[...].astype(F32)
    sig = jax.nn.sigmoid(gf)
    gg = (hf * uact[...].astype(F32) * sig * (1.0 + gf * (1.0 - sig))).astype(BF)
    ug = (hf * gf * sig).astype(BF)
    G[q, 0] = gg
    G[q, 1] = ug

    zcp = [{}, {}]

    def ag_start(h):
        for cp in xcp[h]:
            cp.wait_recv()
        t = tts[h]
        for d in (1, 7, 2, 6, 3, 5, 4):
            zcp[h][d] = send(
                t.at[c, y, 0], t.at[c, y, static_slot(-d)], dev_z(d)
            )

    groups = ((0, 1, ()), (1, 3, (1, 7)), (3, 8, (2, 6, 3, 5, 4)))
    ycp = [{}, {}]
    ocp = [{}, {}]
    scp = [[], []]

    def ag_y(h, gi):
        s0, s1, ds = groups[gi]
        for d in ds:
            zcp[h][d].wait_recv()
        t = tts[h]
        src = t.at[c, y, pl.ds(s0, s1 - s0)]
        ycp[h][gi] = (send(src, src, dev_yp), send(src, src, dev_ym))

    def ag_o(h, gi):
        s0, s1, _ = groups[gi]
        t = tts[h]
        ycp[h][gi][0].wait_recv()
        a = t.at[c, ym, pl.ds(s0, s1 - s0), pl.ds(0, 2)]
        first = send(a, a, dev_yp)
        ycp[h][gi][1].wait_recv()
        b = t.at[c, yp, pl.ds(s0, s1 - s0), pl.ds(2, 2)]
        ocp[h][gi] = (first, send(b, b, dev_ym))

    def ag_sib(h, col):
        r = tts[h].at[c, col]
        scp[h].append(send(r, r, dev_sib))

    ag_start(0)
    ag_y(0, 0)
    for d in (1, 3, 2):
        to = q
        send(G.at[q], G.at[to], dev_x(d))
    gcp = sent[-3:]
    ag_start(1)

    lane = lax.broadcasted_iota(jnp.int32, (2, NM, 128), 2)
    for j in range(2):
        pick = lane == 2 * m + j
        mk = jnp.sum(jnp.where(pick, mask_ref[...], 0).astype(F32), axis=2, keepdims=True)
        ex = jnp.sum(jnp.where(pick, exp_ref[...], 0).astype(F32), axis=2, keepdims=True)
        mkb = jnp.broadcast_to(mk, (2, NM, 128))
        facx[:, j] = mkb * jnp.exp2(-jnp.broadcast_to(ex, (2, NM, 128)))
        wm[:, :, 128 * j : 128 * (j + 1)] = mkb
    for w in range(2):
        row = perm_ref[w, m]
        mrow = mask_ref[w, pl.ds(row, 1), :].astype(F32)
        erow = exp_ref[w, pl.ds(row, 1), :].astype(F32)
        fac_ref[w : w + 1, :] = mrow * jnp.exp2(erow)

    GT[0:256] = gg.T
    GT[256:512] = ug.T
    for cp in wloads:
        cp.wait()

    def ig_chunk(yy):
        def step(i, carry):
            blk = yy * 16 + i * 8
            rows = pl.ds(pl.multiple_of(blk * 128, 1024), 1024)
            acc = None
            for w, wref in enumerate((wg, wu)):
                mrows = wm[w, pl.ds(pl.multiple_of(blk, 8), 8), :].astype(BF)
                wv = wref[rows, :].reshape(8, 128, 256) * mrows[:, None, :]
                r = jnp.dot(
                    wv.reshape(1024, 256), GT[256 * w : 256 * (w + 1)],
                    preferred_element_type=F32,
                )
                acc = r if acc is None else acc + r
            acc = acc.astype(BF).reshape(4, 2, 128, 256)
            for cc in range(2):
                part[cc, yy, pl.ds(i * 4, 4)] = acc[:, cc]
            return carry

        lax.fori_loop(0, 2, step, 0)
        return send(part.at[1 - c, yy], crecv.at[yy], dev_sib)

    ccp = {}
    ccp["o"] = ig_chunk(yo)
    ag_y(0, 1)
    ccp["p"] = ig_chunk(yp)
    ag_y(0, 2)
    ag_sib(0, y)
    ag_y(1, 0)
    ag_o(0, 0)
    ccp["m"] = ig_chunk(ym)
    ag_y(1, 1)
    ag_o(0, 1)
    ccp["s"] = ig_chunk(y)

    def csum(yy):
        for zz in range(NZ):
            v = part[c, yy, zz].astype(F32) + crecv[yy, zz].astype(F32)
            ysum[yy, zz] = v.astype(BF)

    ag_y(1, 2)
    ag_sib(1, y)
    ag_o(0, 2)
    ag_sib(0, ym)
    ag_sib(0, yp)

    ccp["o"].wait_recv()
    csum(yo)
    rcpA = send(ysum.at[yo, pl.ds(0, 4)], yrA, dev_yp)
    rcpB = send(ysum.at[yo, pl.ds(4, 4)], yrB, dev_ym)

    ag_o(1, 0)
    ag_o(1, 1)
    for gi in range(3):
        ocp[0][gi][0].wait_recv()
        ocp[0][gi][1].wait_recv()
    ag_sib(0, yo)
    ag_o(1, 2)
    ag_sib(1, ym)
    ag_sib(1, yp)
    for cp in gcp:
        cp.wait_recv()
    for cp in scp[0]:
        cp.wait_recv()

    def wgrad(h):
        t = tts[h]

        def group(gi, carry):
            for w in range(2):
                def gather(i, carry2):
                    k = lax.rem(m + gi * 16 + i, NM)
                    b = perm_ref[w, k]
                    cc = lax.rem(b, NC)
                    zz = lax.rem(lax.div(b, NC), NZ)
                    yy = lax.div(b, NC * NZ)
                    o = lax.rem(zz + NZ - z, NZ)
                    rows = pl.ds(pl.multiple_of(i * HALF, HALF), HALF)
                    lhs[w, :, rows, :] = t[cc, yy, slot_of(o)]
                    for j in range(2):
                        fs[w, j, rows, :] = jnp.broadcast_to(
                            facx[w, j, pl.ds(b, 1), :], (HALF, 128)
                        )
                    return carry2

                lax.fori_loop(0, 16, gather, 0, unroll=True)
                tot = None
                for p in range(NX):
                    r = jnp.dot(lhs[w, p], G[p, w], preferred_element_type=F32)
                    v = r[:, :128] * fs[w, 0] + r[:, 128:] * fs[w, 1]
                    v = jnp.clip(v, -1.0, 1.0).astype(BF).astype(F32)
                    tot = v if tot is None else tot + v
                abuf[h, pl.ds(gi * 16, 16), w] = tot.astype(BF).reshape(16, HALF, 128)

            def push(i, carry2):
                k = lax.rem(m + i, NM)

                @pl.when(i > 0)
                def _():
                    pltpu.make_async_remote_copy(
                        src_ref=abuf.at[h, i], dst_ref=recv_ref.at[h, m],
                        send_sem=a_ss.at[h], recv_sem=a_rs.at[h],
                        device_id=(q, k), device_id_type=MESH,
                    ).start()

                return carry2

            lax.fori_loop(gi * 16, gi * 16 + 16, push, 0)
            return carry

        lax.fori_loop(0, 4, group, 0)

    wgrad(0)
    own = []
    cp = pltpu.make_async_copy(abuf.at[0, 0], recv_ref.at[0, m], lsem.at[6])
    cp.start()
    own.append(cp)

    ccp["p"].wait_recv()
    ccp["m"].wait_recv()
    csum(yp)
    csum(ym)
    rcpA.wait_recv()
    for i in range(4):
        ysum[yp, i] = (ysum[yp, i].astype(F32) + yrA[i].astype(F32)).astype(BF)
    r2p = send(ysum.at[yp], yr2m, dev_yp)
    rcpB.wait_recv()
    for i in range(4):
        ysum[ym, 4 + i] = (ysum[ym, 4 + i].astype(F32) + yrB[i].astype(F32)).astype(BF)
    r2m = send(ysum.at[ym], yr2p, dev_ym)

    for gi in range(3):
        ocp[1][gi][0].wait_recv()
        ocp[1][gi][1].wait_recv()
    ag_sib(1, yo)
    for cp in scp[1]:
        cp.wait_recv()
    wgrad(1)
    cp = pltpu.make_async_copy(abuf.at[1, 0], recv_ref.at[1, m], lsem.at[7])
    cp.start()
    own.append(cp)

    ccp["s"].wait_recv()
    r2p.wait_recv()
    r2m.wait_recv()
    for i in range(NZ):
        v = part[c, y, i].astype(F32) + crecv[y, i].astype(F32)
        v = v + yr2m[i].astype(F32) + yr2p[i].astype(F32)
        ysum[y, i] = v.astype(BF)
    zc = []
    for d in range(1, NZ):
        zc.append(send(ysum.at[y, lax.rem(z + d, NZ)], zr.at[d - 1], dev_z(d)))
    tot = ysum[y, z].astype(F32)
    for d in range(1, NZ):
        zc[d - 1].wait_recv()
        tot = tot + zr[d - 1].astype(F32)
    ig_ref[...] = tot.T.astype(BF)

    for cp in own:
        cp.wait()
    for h in range(2):
        done = pltpu.make_async_remote_copy(
            src_ref=abuf.at[h, pl.ds(1, NM - 1)], dst_ref=recv_ref.at[h, pl.ds(0, NM - 1)],
            send_sem=a_ss.at[h], recv_sem=a_rs.at[h], device_id=dev_sib, device_id_type=MESH,
        )
        done.wait_recv()
        done.wait_send()
    for cp in sent:
        cp.wait_send()


def expand(recv_ref, fac_ref, out_ref):
    g = pl.program_id(0)
    for s in range(8):
        for w in range(2):
            for h in range(2):
                v = recv_ref[h, s, w].astype(F32)
                for j in range(2):
                    col = (s * 2 + j) * 128
                    f = fac_ref[w, (g * 8 + s) * 2 + j]
                    out_ref[w, h * HALF : (h + 1) * HALF, col : col + 128] = v * f


def body(tokens, gate_act, up_act, hidden_grad, gate_weight, up_weight, block_mask, row_perm, scale_exp):
    any_spec = pl.BlockSpec(memory_space=pl.ANY)
    vm = pl.BlockSpec(memory_space=pltpu.VMEM)
    sm = pl.BlockSpec(memory_space=pltpu.SMEM)
    V = pltpu.VMEM
    tt = V((2, NY, NZ, NX, HALF, 256), BF)
    ig, recv, fac = pl.pallas_call(
        kernel,
        out_shape=(
            jax.ShapeDtypeStruct((256, 128), BF),
            jax.ShapeDtypeStruct((2, NM, 2, HALF, 128), BF),
            jax.ShapeDtypeStruct((2, 128), F32),
        ),
        in_specs=[any_spec] * 6 + [vm, sm, vm],
        out_specs=(vm, any_spec, vm),
        scratch_shapes=[
            V((256, 128), BF), V((256, 256), BF), V((256, 256), BF), V((256, 256), BF),
            V((8192, 256), BF), V((8192, 256), BF),
            V((2, NX, HALF, 256), BF), tt, tt,
            V((NX, 2, 256, 256), BF), V((512, 256), BF),
            V((2, NM, 256), F32), V((2, 2, NM, 128), F32),
            V((2, NX, 256, 256), BF), V((2, 2, 256, 128), F32),
            V((2, NM, 2, HALF, 128), BF),
            V((2, NY, NZ, 128, 256), BF), V((NY, NZ, 128, 256), BF), V((NY, NZ, 128, 256), BF),
            V((4, 128, 256), BF), V((4, 128, 256), BF), V((NZ, 128, 256), BF), V((NZ, 128, 256), BF),
            V((NZ - 1, 128, 256), BF),
            pltpu.SemaphoreType.DMA((N_SEM,)), pltpu.SemaphoreType.DMA((N_SEM,)),
            pltpu.SemaphoreType.DMA((2,)), pltpu.SemaphoreType.DMA((2,)),
            pltpu.SemaphoreType.DMA((8,)),
        ],
        compiler_params=pltpu.CompilerParams(
            collective_id=0, has_side_effects=True, vmem_limit_bytes=56 << 20
        ),
        name="grads",
    )(tokens, gate_act, up_act, hidden_grad, gate_weight, up_weight, block_mask, row_perm, scale_exp)
    out = pl.pallas_call(
        expand,
        grid=(8,),
        out_shape=jax.ShapeDtypeStruct((2, 32, 16384), F32),
        in_specs=[pl.BlockSpec((2, 8, 2, HALF, 128), lambda i: (0, i, 0, 0, 0)), sm],
        out_specs=pl.BlockSpec((2, 32, 2048), lambda i: (0, 0, i)),
        name="expand",
    )(recv, fac)
    return ig, out


def solution(mesh):
    act = P("dp", "mp")
    weight = P(None, "mp")
    in_specs = (act, act, act, act, weight, weight, P(), P(), P())
    out_specs = (act, P(None, ("mp", "dp"), None))
    return jax.shard_map(body, mesh=mesh, in_specs=in_specs, out_specs=out_specs, check_vma=False)
```

time: 641 us -> 93.2 us (0.15)
  waiting for transfers between devices: 394 us -> 0 us
  local copies, waits for them, and re-layouts: 115 us -> 0.63 us
  other arithmetic: 96.7 us -> 0 us
  Pallas kernels: 0 us -> 91.7 us
  between operations: 14.6 us -> 0.65 us
  matrix products: 10.4 us -> 0 us
  starting transfers between devices: 8.86 us -> 0 us
    all_to_all x1 -> x0, waiting for transfers between devices: 179 us -> none  [body(): moved = lax.all_to_all(owned, 'mp', split_axis=1, concat_axis=2, tiled=True)]
    unnamed x4 -> x0, waiting for transfers between devices: 149 us -> none
    pallas_call x0 -> x2, Pallas kernels: none -> 91.7 us  [the longest x1 85.8 us: body(): pl.pallas_call(kernel, out_shape=(jax.ShapeDtypeStruct((256, 128), BF), j...]
    all_gather x1 -> x0, waiting for transfers between devices: 65.9 us -> none  [body(): lax.all_gather(tokens, 'mp', axis=1, tiled=True)]
    select_n x2 -> x0, other arithmetic: 63.5 us -> none  [the longest x1 63.5 us: body(): jnp.take_along_axis(clipped, row_perm[:, :, None, None], axis=1)]
    all_to_all x3 -> x0, local copies, waits for them, and re-layouts: 41 us -> none  [body(): moved = lax.all_to_all(owned, 'mp', split_axis=1, concat_axis=2, tiled=True)]
    another operation x4 -> x0, local copies, waits for them, and re-layouts: 31.8 us -> none  [the longest x2 18 us: body(): jnp.stack([full_grads[:, :width], full_grads[:, width:]])]
    mul x3 -> x0, other arithmetic: 20.8 us -> none  [the longest x1 15.6 us: body(): stacked * mask_factor.astype(jnp.bfloat16)]
  transfers between devices with their start and end apart: 4 -> 0, of which waited for: 3 -> 0; matrix products, arithmetic and copies ran while one was open for 15% -> 0% of each run, Pallas kernels for 0% -> 0%
where the time goes in v1:
time: 93.2 us; the launch traced here: 93 us
  Pallas kernels  91.7 us (98%)
    pallas_call x1, Pallas kernels, body(): pl.pallas_call(kernel, out_shape=(jax.ShapeDtypeStruct((256, 128), BF), j...  85.8 us
    pallas_call x1, Pallas kernels, body(): pl.pallas_call(expand, grid=(8,), out_shape=jax.ShapeDtypeStruct((2, 32,...  5.91 us

profile of v1, /device:TPU:1, one launch (start us, length us, event | category | flops | bytes accessed | tf_op | source)
XLA Modules:
  0.0 93.0 jit_solution(16507179823730567857)
XLA Ops:
  0.6 85.8 %grads.1 = (bf16[256,128]{1,0:T(8,128)(2,1)}, bf16[2,64,2,16,128]{4,3,2,1,0:T(8,128)(2,1)}, f32[2,128]{1,0:T(2,128)}) custom-call(bf16[256,128]{1,0:T(8,128)(2,1)} %tok_ref.1, bf16[256,256]{1,0:T(8,128)(2,1)} %g_ref.1, bf16[256,256]{1,0:T(8,128)(2,1)} %u_ref.1, bf16[256,256]{1,0:T(8,128)(2,1)} %h_ref.1, bf16[8192,256]{1,0:T(8,128)(2,1)} %wg_ref.1, ...), custom_call_target="tpu_custom_call" | custom-call | tf_op jit(solution)/shard_map/grads/pallas_call | solution.py:371
  86.4 0.0 copy-start
  86.4 5.9 %expand.1 = f32[2,32,16384]{2,1,0:T(8,128)} custom-call(bf16[2,64,2,16,128]{4,3,2,1,0:T(8,128)(2,1)} %get-tuple-element.6.recv_ref, f32[2,128]{1,0:T(2,128)} %get-tuple-element.7.fac_ref), custom_call_target="tpu_custom_call" | custom-call | tf_op jit(solution)/shard_map/expand/pallas_call | solution.py:400
  92.3 0.0 copy-done
  92.3 0.6 copy.12
Async XLA Ops:
  86.4 5.9 %copy-start = (bf16[256,128]{1,0:T(8,128)(2,1)S(1)}, bf16[256,128]{1,0:T(8,128)(2,1)}, u32[]{:S(2)}) copy-start(bf16[256,128]{1,0:T(8,128)(2,1)} %get-tuple-element.10) | copy-start | bytes 196612

commit v2 on v1

v2 whole, which is shorter than its diff:
```python
import jax
import jax.numpy as jnp
from jax import lax
from jax.experimental import pallas as pl
from jax.experimental.pallas import tpu as pltpu
from jax.sharding import PartitionSpec as P

BF = jnp.bfloat16
F32 = jnp.float32
MESH = pl.DeviceIdType.MESH
NX, NY, NZ, NC = 4, 4, 8, 2
NM = NY * NZ * NC
HALF = 16
N_SEM = 96


def slot_of(o):
    return jnp.where(o <= 3, 2 * o, jnp.where(o == 4, 7, 2 * (8 - o) - 1))


def static_slot(o):
    o %= 8
    return 2 * o if o <= 3 else (7 if o == 4 else 2 * (8 - o) - 1)


SCHEDULE = (
    ("xt",), ("ga",), ("zs",), ("y", 0), ("ys",), ("gx",), ("mk",), ("il",), ("i", "o"), ("i", "p"),
    ("y", 1), ("i", "m"), ("i", "s"), ("k", 1), ("bk", 0), ("c", "o"), ("r1",), ("o", 0), ("y", 2),
    ("b", "s"), ("k", 2), ("bk", 1), ("o", 1), ("c", "p"), ("c", "m"), ("c", "s"), ("o", 2),
    ("k", 3), ("bk", 2), ("r2",), ("b", "m"), ("b", "p"), ("k", 4), ("bk", 3), ("b", "o"), ("w", 0),
    ("bk", 4), ("w", 1, 0, 1), ("rz", 4), ("w", 1, 1, 2), ("rz", 3), ("w", 1, 2, 3), ("rz", 2),
    ("w", 1, 3, 4), ("rz", 1), ("rz", 0),
)


def kernel(
    tok_ref, g_ref, u_ref, h_ref, wg_ref, wu_ref, mask_ref, perm_ref, exp_ref,
    ig_ref, recv_ref, fac_ref,
    tok, gact, uact, hgrad, wg, wu, xsrc, tt0, tt1, G, GT, wm, facx, lhs, fs, abuf,
    part, crecv, ysum, yrA, yrB, yr2m, yr2p, zra, zrb, zr,
    ss, rs, a_ss, a_rs, lsem,
):
    q = lax.axis_index("dp")
    m = lax.axis_index("mp")
    c = lax.rem(m, NC)
    z = lax.rem(lax.div(m, NC), NZ)
    y = lax.div(m, NC * NZ)
    yp, ym, yo = lax.rem(y + 1, NY), lax.rem(y + 3, NY), lax.rem(y + 2, NY)

    def mp_of(yy, zz, cc):
        return (yy * NZ + zz) * NC + cc

    dev_yp, dev_ym = (q, mp_of(yp, z, c)), (q, mp_of(ym, z, c))
    dev_sib = (q, mp_of(y, z, 1 - c))

    def dev_z(d):
        return (q, mp_of(y, lax.rem(z + d, NZ), c))

    def dev_x(d):
        return (lax.rem(q + d, NX), m)

    loads = []
    for i, (src, dst) in enumerate(
        ((tok_ref, tok), (g_ref, gact), (u_ref, uact), (h_ref, hgrad))
    ):
        cp = pltpu.make_async_copy(src, dst, lsem.at[i])
        cp.start()
        loads.append(cp)
    wloads = []
    for i, (src, dst) in enumerate(((wg_ref, wg), (wu_ref, wu))):
        cp = pltpu.make_async_copy(src, dst, lsem.at[4 + i])
        cp.start()
        wloads.append(cp)

    barrier = pltpu.get_barrier_semaphore()

    partners = [dev_sib] + [dev_z(d) for d in range(1, NZ)] + [dev_x(d) for d in range(1, NX)]
    partners += [(q, mp_of(lax.rem(y + d, NY), z, c)) for d in range(1, NY)]
    for dev in partners:
        pl.semaphore_signal(barrier, inc=1, device_id=dev, device_id_type=MESH)

    sent = []

    class Remote:
        def __init__(self, src, dst, dev):
            i = len(sent)
            self.copy = pltpu.make_async_remote_copy(
                src_ref=src, dst_ref=dst, send_sem=ss.at[i], recv_sem=rs.at[i],
                device_id=dev, device_id_type=MESH,
            )
            self.copy.start()
            self.pending = True
            sent.append(self)

        def recv(self):
            if self.pending:
                self.copy.wait_recv()
                self.pending = False

    X, Z, Y, O, K, S, I, R = ({} for _ in range(8))
    own = []
    cols = {"s": y, "p": yp, "m": ym, "o": yo}

    def own_block(h):
        return tt0.at[c, y, 0] if h == 0 else tt1.at[c, 0, y]

    def x_tokens():
        loads[0].wait()
        tok_t = tok[...].T
        for h in range(2):
            for k in range(NX):
                xsrc[h, k] = tok_t[32 * k + HALF * h : 32 * k + HALF * (h + 1), :]
            own_block(h)[q] = xsrc[h, q]
        pl.semaphore_wait(barrier, len(partners))
        for h in range(2):
            for d in (1, 3, 2):
                to = lax.rem(q + d, NX)
                X[h, d] = Remote(xsrc.at[h, to], own_block(h).at[q], dev_x(d))

    def z_start():
        for d in (1, 3, 2):
            X[0, d].recv()
        for d in (1, 7, 2, 6, 3, 5, 4):
            Z[d] = Remote(tt0.at[c, y, 0], tt0.at[c, y, static_slot(-d)], dev_z(d))

    groups = ((0, 1, ()), (1, 3, (1, 7)), (3, 8, (2, 6, 3, 5, 4)))

    def y_first(g):
        s0, s1, ds = groups[g]
        for d in ds:
            Z[d].recv()
        r = tt0.at[c, y, pl.ds(s0, s1 - s0)]
        Y[g, "m"] = Remote(r, r, dev_yp)
        Y[g, "p"] = Remote(r, r, dev_ym)

    def y_second(g):
        s0, s1, _ = groups[g]
        Y[g, "m"].recv()
        r = tt0.at[c, ym, pl.ds(s0, s1 - s0), pl.ds(0, 2)]
        O[g, 0] = Remote(r, r, dev_yp)
        Y[g, "p"].recv()
        r = tt0.at[c, yp, pl.ds(s0, s1 - s0), pl.ds(2, 2)]
        O[g, 1] = Remote(r, r, dev_ym)

    def sibling(col):
        for g in range(3):
            if col == "o":
                O[g, 0].recv()
                O[g, 1].recv()
            elif col != "s":
                Y[g, col].recv()
        r = tt0.at[c, cols[col]]
        S[0, col] = Remote(r, r, dev_sib)

    def y_start():
        for d in (1, 3, 2):
            X[1, d].recv()
        r = own_block(1)
        for d in (1, 3, 2):
            Y["k", d] = Remote(r, r, (q, mp_of(lax.rem(y + d, NY), z, c)))

    def k_recv(step):
        for way in (1, -1):
            for n in range(2):
                if (step, way, n) in K:
                    K[step, way, n].recv()

    def k_step(step):
        if step == 1:
            for d in (1, 3, 2):
                Y["k", d].recv()
        for n in range(2):
            for way in (1, -1):
                if step == 4 and (way == 1) != (n == 0):
                    continue
                if step > 1:
                    K[step - 1, way, n].recv()
                half = pl.ds(2 * n, 2)
                src = tt1.at[c, static_slot(-way * (step - 1)), half]
                dst = tt1.at[c, static_slot(-way * step), half]
                K[step, way, n] = Remote(src, dst, dev_z(way % NZ))

    def k_sibling(g):
        k_recv(g)
        s0, s1 = ((0, 1), (1, 3), (3, 5), (5, 7), (7, 8))[g]
        r = tt1.at[c, pl.ds(s0, s1 - s0)]
        S[1, g] = Remote(r, r, dev_sib)

    def act_grads():
        for cp in loads[1:]:
            cp.wait()
        gf = gact[...].astype(F32)
        hf = hgrad[...].astype(F32)
        sig = jax.nn.sigmoid(gf)
        gg = (hf * uact[...].astype(F32) * sig * (1.0 + gf * (1.0 - sig))).astype(BF)
        ug = (hf * gf * sig).astype(BF)
        G[q, 0] = gg
        G[q, 1] = ug
        GT[0:256] = gg.T
        GT[256:512] = ug.T

    def x_grads():
        for d in (1, 3, 2):
            X["g", d] = Remote(G.at[q], G.at[q], dev_x(d))

    def masks():
        lane = lax.broadcasted_iota(jnp.int32, (2, NM, 128), 2)
        for j in range(2):
            pick = lane == 2 * m + j
            mk = jnp.sum(jnp.where(pick, mask_ref[...], 0).astype(F32), axis=2, keepdims=True)
            ex = jnp.sum(jnp.where(pick, exp_ref[...], 0).astype(F32), axis=2, keepdims=True)
            mkb = jnp.broadcast_to(mk, (2, NM, 128))
            facx[:, j] = mkb * jnp.exp2(-jnp.broadcast_to(ex, (2, NM, 128)))
            wm[:, :, 128 * j : 128 * (j + 1)] = mkb
        for w in range(2):
            row = perm_ref[w, m]
            mrow = mask_ref[w, pl.ds(row, 1), :].astype(F32)
            erow = exp_ref[w, pl.ds(row, 1), :].astype(F32)
            fac_ref[w : w + 1, :] = mrow * jnp.exp2(erow)

    def ig_load():
        for cp in wloads:
            cp.wait()

    def ig_chunk(col):
        yy = cols[col]

        def step(i, carry):
            blk = yy * 16 + i * 8
            rows = pl.ds(pl.multiple_of(blk * 128, 1024), 1024)
            acc = None
            for w, wref in enumerate((wg, wu)):
                mrows = wm[w, pl.ds(pl.multiple_of(blk, 8), 8), :].astype(BF)
                wv = wref[rows, :].reshape(8, 128, 256) * mrows[:, None, :]
                r = jnp.dot(
                    wv.reshape(1024, 256), GT[256 * w : 256 * (w + 1)],
                    preferred_element_type=F32,
                )
                acc = r if acc is None else acc + r
            acc = acc.astype(BF).reshape(4, 2, 128, 256)
            for cc in range(2):
                part[cc, yy, pl.ds(i * 4, 4)] = acc[:, cc]
            return carry

        lax.fori_loop(0, 2, step, 0)
        I[col] = Remote(part.at[1 - c, yy], crecv.at[yy], dev_sib)

    def core_sum(col):
        yy = cols[col]
        I[col].recv()
        for zz in range(NZ):
            v = part[c, yy, zz].astype(F32) + crecv[yy, zz].astype(F32)
            ysum[yy, zz] = v.astype(BF)

    def add(dst, src):
        dst[...] = (dst[...].astype(F32) + src[...].astype(F32)).astype(BF)

    def rs_first():
        R["A"] = Remote(ysum.at[yo, pl.ds(0, 4)], yrA, dev_yp)
        R["B"] = Remote(ysum.at[yo, pl.ds(4, 4)], yrB, dev_ym)

    def rs_second():
        R["A"].recv()
        for i in range(4):
            add(ysum.at[yp, i], yrA.at[i])
        R["m"] = Remote(ysum.at[yp], yr2m, dev_yp)
        R["B"].recv()
        for i in range(4):
            add(ysum.at[ym, 4 + i], yrB.at[i])
        R["p"] = Remote(ysum.at[ym], yr2p, dev_ym)

    def rs_z(step):
        if step == 4:
            R["m"].recv()
            R["p"].recv()
            for d in (4, 3, 5, 2, 6, 1, 7, 0):
                i = lax.rem(z + d, NZ)
                v = ysum[y, i].astype(F32) + yr2m[i].astype(F32) + yr2p[i].astype(F32)
                ysum[y, i] = v.astype(BF)
                if d == 4:
                    R["u", 4] = Remote(ysum.at[y, i, pl.ds(0, 64)], zra, dev_z(1))
                    R["d", 4] = Remote(ysum.at[y, i, pl.ds(64, 64)], zrb, dev_z(NZ - 1))
        elif step > 0:
            d = step
            for way, n, half, end in (("u", 0, zra, 1), ("d", 1, zrb, NZ - 1)):
                i = lax.rem(z + (d if n == 0 else NZ - d), NZ)
                R[way, d + 1].recv()
                if d == 3:
                    add(ysum.at[y, i, pl.ds(64 * n, 64)], half)
                else:
                    add(ysum.at[y, i], zr.at[n, 2 - d])
                R[way, d] = Remote(ysum.at[y, i], zr.at[n, 3 - d], dev_z(end))
        else:
            R["u", 1].recv()
            R["d", 1].recv()
            ig_ref[...] = ysum[y, z].astype(F32) + zr[0, 2].astype(F32) + zr[1, 2].astype(F32)

    def wgrad(h, g0=0, g1=4):
        for d in (1, 3, 2):
            X["g", d].recv()
        for (half, _), r in S.items():
            if half == h:
                r.recv()

        def group(gi, carry):
            for w in range(2):
                def gather(i, carry2):
                    k = lax.rem(m + gi * 16 + i, NM)
                    b = perm_ref[w, k]
                    cc = lax.rem(b, NC)
                    zz = lax.rem(lax.div(b, NC), NZ)
                    yy = lax.div(b, NC * NZ)
                    o = lax.rem(zz + NZ - z, NZ)
                    rows = pl.ds(pl.multiple_of(i * HALF, HALF), HALF)
                    if h == 0:
                        lhs[w, :, rows, :] = tt0[cc, yy, slot_of(o)]
                    else:
                        lhs[w, :, rows, :] = tt1[cc, slot_of(o), yy]
                    for j in range(2):
                        fs[w, j, rows, :] = jnp.broadcast_to(
                            facx[w, j, pl.ds(b, 1), :], (HALF, 128)
                        )
                    return carry2

                lax.fori_loop(0, 16, gather, 0, unroll=True)
                tot = None
                for p in range(NX):
                    r = jnp.dot(lhs[w, p], G[p, w], preferred_element_type=F32)
                    v = r[:, :128] * fs[w, 0] + r[:, 128:] * fs[w, 1]
                    v = jnp.clip(v, -1.0, 1.0).astype(BF).astype(F32)
                    tot = v if tot is None else tot + v
                abuf[h, pl.ds(gi * 16, 16), w] = tot.astype(BF).reshape(16, HALF, 128)

            def push(i, carry2):
                k = lax.rem(m + i, NM)

                @pl.when(i > 0)
                def _():
                    pltpu.make_async_remote_copy(
                        src_ref=abuf.at[h, i], dst_ref=recv_ref.at[h, m],
                        send_sem=a_ss.at[h], recv_sem=a_rs.at[h],
                        device_id=(q, k), device_id_type=MESH,
                    ).start()

                return carry2

            lax.fori_loop(gi * 16, gi * 16 + 16, push, 0)
            return carry

        lax.fori_loop(g0, g1, group, 0)
        if g0 == 0:
            cp = pltpu.make_async_copy(abuf.at[h, 0], recv_ref.at[h, m], lsem.at[6 + h])
            cp.start()
            own.append((h, cp))

    ops = {
        "xt": x_tokens, "zs": z_start, "y": y_first, "o": y_second, "b": sibling,
        "ys": y_start, "k": k_step, "bk": k_sibling,
        "ga": act_grads, "gx": x_grads, "mk": masks, "il": ig_load, "i": ig_chunk,
        "c": core_sum, "r1": rs_first, "r2": rs_second, "rz": rs_z, "w": wgrad,
    }
    for name, *args in SCHEDULE:
        ops[name](*args)

    for h, cp in own:
        cp.wait()
        done = pltpu.make_async_remote_copy(
            src_ref=abuf.at[h, pl.ds(1, NM - 1)], dst_ref=recv_ref.at[h, pl.ds(0, NM - 1)],
            send_sem=a_ss.at[h], recv_sem=a_rs.at[h], device_id=dev_sib, device_id_type=MESH,
        )
        done.wait_recv()
        done.wait_send()
    for r in sent:
        r.recv()
        r.copy.wait_send()


def expand(recv_ref, fac_ref, igt_ref, out_ref, ig_ref, rbuf, obuf, lsem, osem):
    n = 4
    per = NM // n
    ins = []
    for g in range(n):
        part = pl.ds(g * per, per)
        cp = pltpu.make_async_copy(recv_ref.at[:, part], rbuf.at[:, part], lsem.at[g])
        cp.start()
        ins.append(cp)
    ig_ref[...] = igt_ref[...].T.astype(BF)
    outs = []
    for g in range(n):
        ins[g].wait()
        for i in range(g * per, (g + 1) * per):
            for w in range(2):
                for h in range(2):
                    v = rbuf[h, i, w].astype(F32)
                    for j in range(2):
                        col = (i * 2 + j) * 128
                        f = fac_ref[w, i * 2 + j]
                        obuf[w, h * HALF : (h + 1) * HALF, col : col + 128] = v * f
        cols = pl.ds(g * per * 256, per * 256)
        cp = pltpu.make_async_copy(obuf.at[:, :, cols], out_ref.at[:, :, cols], osem.at[g])
        cp.start()
        outs.append(cp)
    for cp in outs:
        cp.wait()


def body(tokens, gate_act, up_act, hidden_grad, gate_weight, up_weight, block_mask, row_perm, scale_exp):
    any_spec = pl.BlockSpec(memory_space=pl.ANY)
    vm = pl.BlockSpec(memory_space=pltpu.VMEM)
    sm = pl.BlockSpec(memory_space=pltpu.SMEM)
    V = pltpu.VMEM
    igt, recv, fac = pl.pallas_call(
        kernel,
        out_shape=(
            jax.ShapeDtypeStruct((128, 256), F32),
            jax.ShapeDtypeStruct((2, NM, 2, HALF, 128), BF),
            jax.ShapeDtypeStruct((2, 128), F32),
        ),
        in_specs=[any_spec] * 6 + [vm, sm, vm],
        out_specs=(vm, any_spec, vm),
        scratch_shapes=[
            V((256, 128), BF), V((256, 256), BF), V((256, 256), BF), V((256, 256), BF),
            V((8192, 256), BF), V((8192, 256), BF),
            V((2, NX, HALF, 256), BF),
            V((2, NY, NZ, NX, HALF, 256), BF), V((2, NZ, NY, NX, HALF, 256), BF),
            V((NX, 2, 256, 256), BF), V((512, 256), BF),
            V((2, NM, 256), F32), V((2, 2, NM, 128), F32),
            V((2, NX, 256, 256), BF), V((2, 2, 256, 128), F32),
            V((2, NM, 2, HALF, 128), BF),
            V((2, NY, NZ, 128, 256), BF), V((NY, NZ, 128, 256), BF), V((NY, NZ, 128, 256), BF),
            V((4, 128, 256), BF), V((4, 128, 256), BF), V((NZ, 128, 256), BF), V((NZ, 128, 256), BF),
            V((64, 256), BF), V((64, 256), BF), V((2, 3, 128, 256), BF),
            pltpu.SemaphoreType.DMA((N_SEM,)), pltpu.SemaphoreType.DMA((N_SEM,)),
            pltpu.SemaphoreType.DMA((2,)), pltpu.SemaphoreType.DMA((2,)),
            pltpu.SemaphoreType.DMA((8,)),
        ],
        compiler_params=pltpu.CompilerParams(
            collective_id=0, has_side_effects=True, vmem_limit_bytes=56 << 20
        ),
        name="grads",
    )(tokens, gate_act, up_act, hidden_grad, gate_weight, up_weight, block_mask, row_perm, scale_exp)
    out, ig = pl.pallas_call(
        expand,
        out_shape=(
            jax.ShapeDtypeStruct((2, 32, 16384), F32),
            jax.ShapeDtypeStruct((256, 128), BF),
        ),
        in_specs=[any_spec, sm, vm],
        out_specs=(any_spec, vm),
        scratch_shapes=[
            V((2, NM, 2, HALF, 128), BF), V((2, 32, 16384), F32),
            pltpu.SemaphoreType.DMA((4,)), pltpu.SemaphoreType.DMA((4,)),
        ],
        compiler_params=pltpu.CompilerParams(vmem_limit_bytes=32 << 20),
        name="expand",
    )(recv, fac, igt)
    return ig, out


def solution(mesh):
    act = P("dp", "mp")
    weight = P(None, "mp")
    in_specs = (act, act, act, act, weight, weight, P(), P(), P())
    out_specs = (act, P(None, ("mp", "dp"), None))
    return jax.shard_map(body, mesh=mesh, in_specs=in_specs, out_specs=out_specs, check_vma=False)
```

time: 93.2 us -> 78.8 us (0.85)
  Pallas kernels: 91.7 us -> 75.2 us
  local copies, waits for them, and re-layouts: 0.63 us -> 2.79 us
    pallas_call x2, Pallas kernels: 91.7 us -> 75.2 us  [the longest x1 71.7 us: body(): pl.pallas_call(kernel, out_shape=(jax.ShapeDtypeStruct((128, 256), F32),...]
    unnamed x3 -> x6, local copies, waits for them, and re-layouts: 0.63 us -> 2.79 us
where the time goes in v2:
time: 78.8 us; the launch traced here: 78.6 us
  Pallas kernels  75.2 us (95%)
  local copies, waits for them, and re-layouts  2.79 us (4%)
    pallas_call x1, Pallas kernels, body(): pl.pallas_call(kernel, out_shape=(jax.ShapeDtypeStruct((128, 256), F32),...  71.7 us
    pallas_call x1, Pallas kernels, body(): pl.pallas_call(expand, out_shape=(jax.ShapeDtypeStruct((2, 32, 16384), F3...  3.5 us
    unnamed x6, local copies, waits for them, and re-layouts  2.79 us

profile of v2, /device:TPU:1, one launch (start us, length us, event | category | flops | bytes accessed | tf_op | source)
XLA Modules:
  0.0 78.6 jit_solution(16693431899484907191)
XLA Ops:
  0.6 71.7 %grads.1 = (f32[128,256]{1,0:T(8,128)}, bf16[2,64,2,16,128]{4,3,2,1,0:T(8,128)(2,1)}, f32[2,128]{1,0:T(2,128)}) custom-call(bf16[256,128]{1,0:T(8,128)(2,1)} %tok_ref.1, bf16[256,256]{1,0:T(8,128)(2,1)} %g_ref.1, bf16[256,256]{1,0:T(8,128)(2,1)} %u_ref.1, bf16[256,256]{1,0:T(8,128)(2,1)} %h_ref.1, bf16[8192,256]{1,0:T(8,128)(2,1)} %wg_ref.1, ...), custom_call_target="tpu_custom_call" | custom-call | tf_op jit(solution)/shard_map/grads/pallas_call | solution.py:412
  72.3 0.0 copy-start
  72.3 1.2 %copy-done = bf16[2,64,2,16,128]{4,3,2,1,0:T(8,128)(2,1)S(1)} copy-done((bf16[2,64,2,16,128]{4,3,2,1,0:T(8,128)(2,1)S(1)}, bf16[2,64,2,16,128]{4,3,2,1,0:T(8,128)(2,1)}, u32[]{:S(2)}) %copy-start) | copy-done | bytes 1048600
  73.5 0.0 copy-start.1
  73.5 0.9 %copy-done.1 = f32[128,256]{1,0:T(8,128)S(1)} copy-done((f32[128,256]{1,0:T(8,128)S(1)}, f32[128,256]{1,0:T(8,128)}, u32[]{:S(2)}) %copy-start.1) | copy-done | bytes 131096
  74.4 0.0 copy-start.2
  74.4 0.7 copy-done.2
  75.1 3.5 %expand.1 = (f32[2,32,16384]{2,1,0:T(8,128)}, bf16[256,128]{1,0:T(8,128)(2,1)}) custom-call(bf16[2,64,2,16,128]{4,3,2,1,0:T(8,128)(2,1)S(1)} %copy-done, f32[2,128]{1,0:T(2,128)S(1)} %copy-done.2, f32[128,256]{1,0:T(8,128)S(1)} %copy-done.1), custom_call_target="tpu_custom_call" | custom-call | tf_op jit(solution)/shard_map/expand/pallas_call | solution.py:442
Async XLA Ops:
  72.3 1.2 %copy-start = (bf16[2,64,2,16,128]{4,3,2,1,0:T(8,128)(2,1)S(1)}, bf16[2,64,2,16,128]{4,3,2,1,0:T(8,128)(2,1)}, u32[]{:S(2)}) copy-start(bf16[2,64,2,16,128]{4,3,2,1,0:T(8,128)(2,1)} %get-tuple-element.7.recv_ref) | copy-start | bytes 3145732
  73.5 0.9 %copy-start.1 = (f32[128,256]{1,0:T(8,128)S(1)}, f32[128,256]{1,0:T(8,128)}, u32[]{:S(2)}) copy-start(f32[128,256]{1,0:T(8,128)} %get-tuple-element.9.igt_ref) | copy-start | bytes 393220
  74.4 0.7 copy-start.2

commit v3 on v2

--- a/solution.py
+++ b/solution.py
@@ -24,20 +24,21 @@
 
 
 SCHEDULE = (
-    ("xt",), ("ga",), ("zs",), ("y", 0), ("ys",), ("gx",), ("mk",), ("il",), ("i", "o"), ("i", "p"),
-    ("y", 1), ("i", "m"), ("i", "s"), ("k", 1), ("bk", 0), ("c", "o"), ("r1",), ("o", 0), ("y", 2),
-    ("b", "s"), ("k", 2), ("bk", 1), ("o", 1), ("c", "p"), ("c", "m"), ("c", "s"), ("o", 2),
-    ("k", 3), ("bk", 2), ("r2",), ("b", "m"), ("b", "p"), ("k", 4), ("bk", 3), ("b", "o"), ("w", 0),
-    ("bk", 4), ("w", 1, 0, 1), ("rz", 4), ("w", 1, 1, 2), ("rz", 3), ("w", 1, 2, 3), ("rz", 2),
-    ("w", 1, 3, 4), ("rz", 1), ("rz", 0),
+    ("xt",), ("ga",), ("mk",), ("il",), ("i", "o"), ("i", "p"), ("i", "m"), ("i", "s"), ("zs",),
+    ("y", 0), ("ys",), ("gx",), ("c", "o"), ("r1",), ("y", 1), ("k", 1), ("bk", 0), ("o", 0),
+    ("y", 2), ("b", "s"), ("c", "p"), ("c", "m"), ("c", "s"), ("k", 2), ("bk", 1), ("o", 1),
+    ("o", 2), ("k", 3), ("bk", 2), ("r2",), ("b", "m"), ("b", "p"), ("k", 4), ("bk", 3), ("b", "o"),
+    ("w", 0), ("bk", 4), ("w", 1, 0, 1), ("rz", 4), ("w", 1, 1, 2), ("rz", 3), ("w", 1, 2, 3),
+    ("rz", 2), ("w", 1, 3, 4), ("rz", 1), ("rz", 0),
 )
 
 
 def kernel(
-    tok_ref, g_ref, u_ref, h_ref, wg_ref, wu_ref, mask_ref, perm_ref, exp_ref,
+    tok_ref, g_ref, u_ref, h_ref, wg_ref, wu_ref, mask_hbm, perm_hbm, exp_hbm,
     ig_ref, recv_ref, fac_ref,
+    mask_ref, perm_ref, exp_ref,
     tok, gact, uact, hgrad, wg, wu, xsrc, tt0, tt1, G, GT, wm, facx, lhs, fs, abuf,
-    part, crecv, ysum, yrA, yrB, yr2m, yr2p, zra, zrb, zr,
+    part, crecv, ysum, yrA, yrB, yr2m, yr2p, zra, zrb, zr, zd,
     ss, rs, a_ss, a_rs, lsem,
 ):
     q = lax.axis_index("dp")
@@ -64,6 +65,12 @@
         ((tok_ref, tok), (g_ref, gact), (u_ref, uact), (h_ref, hgrad))
     ):
         cp = pltpu.make_async_copy(src, dst, lsem.at[i])
+        cp.start()
+        loads.append(cp)
+    for i, (src, dst) in enumerate(
+        ((mask_hbm, mask_ref), (perm_hbm, perm_ref), (exp_hbm, exp_ref))
+    ):
+        cp = pltpu.make_async_copy(src, dst, lsem.at[8 + i])
         cp.start()
         loads.append(cp)
     wloads = []
@@ -132,6 +139,13 @@
         r = tt0.at[c, y, pl.ds(s0, s1 - s0)]
         Y[g, "m"] = Remote(r, r, dev_yp)
         Y[g, "p"] = Remote(r, r, dev_ym)
+
+    def y_direct(g):
+        y_first(g)
+        s0, s1, _ = groups[g]
+        r = tt0.at[c, y, pl.ds(s0, s1 - s0)]
+        O[g, 0] = Remote(r, r, (q, mp_of(yo, z, c)))
+        O[g, 1] = O[g, 0]
 
     def y_second(g):
         s0, s1, _ = groups[g]
@@ -187,7 +201,7 @@
         S[1, g] = Remote(r, r, dev_sib)
 
     def act_grads():
-        for cp in loads[1:]:
+        for cp in loads[1:4]:
             cp.wait()
         gf = gact[...].astype(F32)
         hf = hgrad[...].astype(F32)
@@ -204,6 +218,8 @@
             X["g", d] = Remote(G.at[q], G.at[q], dev_x(d))
 
     def masks():
+        for cp in loads[4:]:
+            cp.wait()
         lane = lax.broadcasted_iota(jnp.int32, (2, NM, 128), 2)
         for j in range(2):
             pick = lane == 2 * m + j
@@ -216,7 +232,7 @@
             row = perm_ref[w, m]
             mrow = mask_ref[w, pl.ds(row, 1), :].astype(F32)
             erow = exp_ref[w, pl.ds(row, 1), :].astype(F32)
-            fac_ref[w : w + 1, :] = mrow * jnp.exp2(erow)
+            fac_ref[w] = jnp.broadcast_to(mrow * jnp.exp2(erow), (128, 128)).T
 
     def ig_load():
         for cp in wloads:
@@ -259,20 +275,47 @@
         R["A"] = Remote(ysum.at[yo, pl.ds(0, 4)], yrA, dev_yp)
         R["B"] = Remote(ysum.at[yo, pl.ds(4, 4)], yrB, dev_ym)
 
+    def rs_early():
+        R["eu"] = Remote(ysum.at[yp, pl.ds(4, 4)], yr2m.at[pl.ds(4, 4)], dev_yp)
+        R["ed"] = Remote(ysum.at[ym, pl.ds(0, 4)], yr2p.at[pl.ds(0, 4)], dev_ym)
+
     def rs_second():
         R["A"].recv()
         for i in range(4):
             add(ysum.at[yp, i], yrA.at[i])
-        R["m"] = Remote(ysum.at[yp], yr2m, dev_yp)
+        up, down = (pl.ds(0, 4), pl.ds(4, 4)) if "eu" in R else (pl.ds(0, 8), pl.ds(0, 8))
+        R["m"] = Remote(ysum.at[yp, up], yr2m.at[up], dev_yp)
         R["B"].recv()
         for i in range(4):
             add(ysum.at[ym, 4 + i], yrB.at[i])
-        R["p"] = Remote(ysum.at[ym], yr2p, dev_ym)
+        R["p"] = Remote(ysum.at[ym, down], yr2p.at[down], dev_ym)
+
+    def rs_z_direct():
+        for r in ("eu", "ed", "m", "p"):
+            if r in R:
+                R[r].recv()
+        for d in (4, 3, 5, 2, 6, 1, 7, 0):
+            i = lax.rem(z + d, NZ)
+            v = ysum[y, i].astype(F32) + yr2m[i].astype(F32) + yr2p[i].astype(F32)
+            if d == 0:
+                ig_ref[...] = v
+            else:
+                ysum[y, i] = v.astype(BF)
+                R["z", d] = Remote(ysum.at[y, i], zd.at[d - 1], dev_z(d))
+
+    def rs_final():
+        for d in range(1, NZ):
+            R["z", d].recv()
+        v = ig_ref[...]
+        for d in range(1, NZ):
+            v = v + zd[d - 1].astype(F32)
+        ig_ref[...] = v
 
     def rs_z(step):
         if step == 4:
-            R["m"].recv()
-            R["p"].recv()
+            for r in ("eu", "ed", "m", "p"):
+                if r in R:
+                    R[r].recv()
             for d in (4, 3, 5, 2, 6, 1, 7, 0):
                 i = lax.rem(z + d, NZ)
                 v = ysum[y, i].astype(F32) + yr2m[i].astype(F32) + yr2p[i].astype(F32)
@@ -354,10 +397,11 @@
             own.append((h, cp))
 
     ops = {
-        "xt": x_tokens, "zs": z_start, "y": y_first, "o": y_second, "b": sibling,
+        "xt": x_tokens, "zs": z_start, "y": y_first, "o": y_second, "yd": y_direct, "b": sibling,
         "ys": y_start, "k": k_step, "bk": k_sibling,
         "ga": act_grads, "gx": x_grads, "mk": masks, "il": ig_load, "i": ig_chunk,
-        "c": core_sum, "r1": rs_first, "r2": rs_second, "rz": rs_z, "w": wgrad,
+        "c": core_sum, "r1": rs_first, "re": rs_early, "r2": rs_second,
+        "rd": rs_z_direct, "rf": rs_final, "rz": rs_z, "w": wgrad,
     }
     for name, *args in SCHEDULE:
         ops[name](*args)
@@ -394,7 +438,7 @@
                     v = rbuf[h, i, w].astype(F32)
                     for j in range(2):
                         col = (i * 2 + j) * 128
-                        f = fac_ref[w, i * 2 + j]
+                        f = fac_ref[w, i * 2 + j : i * 2 + j + 1, :]
                         obuf[w, h * HALF : (h + 1) * HALF, col : col + 128] = v * f
         cols = pl.ds(g * per * 256, per * 256)
         cp = pltpu.make_async_copy(obuf.at[:, :, cols], out_ref.at[:, :, cols], osem.at[g])
@@ -407,18 +451,18 @@
 def body(tokens, gate_act, up_act, hidden_grad, gate_weight, up_weight, block_mask, row_perm, scale_exp):
     any_spec = pl.BlockSpec(memory_space=pl.ANY)
     vm = pl.BlockSpec(memory_space=pltpu.VMEM)
-    sm = pl.BlockSpec(memory_space=pltpu.SMEM)
     V = pltpu.VMEM
     igt, recv, fac = pl.pallas_call(
         kernel,
         out_shape=(
-            jax.ShapeDtypeStruct((128, 256), F32),
-            jax.ShapeDtypeStruct((2, NM, 2, HALF, 128), BF),
-            jax.ShapeDtypeStruct((2, 128), F32),
+            V((128, 256), F32),
+            V((2, NM, 2, HALF, 128), BF),
+            V((2, 128, 128), F32),
         ),
-        in_specs=[any_spec] * 6 + [vm, sm, vm],
+        in_specs=[any_spec] * 9,
         out_specs=(vm, any_spec, vm),
         scratch_shapes=[
+            V((2, NM, 128), jnp.int32), pltpu.SMEM((2, NM), jnp.int32), V((2, NM, 128), jnp.int32),
             V((256, 128), BF), V((256, 256), BF), V((256, 256), BF), V((256, 256), BF),
             V((8192, 256), BF), V((8192, 256), BF),
             V((2, NX, HALF, 256), BF),
@@ -430,9 +474,10 @@
             V((2, NY, NZ, 128, 256), BF), V((NY, NZ, 128, 256), BF), V((NY, NZ, 128, 256), BF),
             V((4, 128, 256), BF), V((4, 128, 256), BF), V((NZ, 128, 256), BF), V((NZ, 128, 256), BF),
             V((64, 256), BF), V((64, 256), BF), V((2, 3, 128, 256), BF),
+            V((NZ - 1, 128, 256), BF),
             pltpu.SemaphoreType.DMA((N_SEM,)), pltpu.SemaphoreType.DMA((N_SEM,)),
             pltpu.SemaphoreType.DMA((2,)), pltpu.SemaphoreType.DMA((2,)),
-            pltpu.SemaphoreType.DMA((8,)),
+            pltpu.SemaphoreType.DMA((11,)),
         ],
         compiler_params=pltpu.CompilerParams(
             collective_id=0, has_side_effects=True, vmem_limit_bytes=56 << 20
@@ -445,7 +490,7 @@
             jax.ShapeDtypeStruct((2, 32, 16384), F32),
             jax.ShapeDtypeStruct((256, 128), BF),
         ),
-        in_specs=[any_spec, sm, vm],
+        in_specs=[any_spec, vm, vm],
         out_specs=(any_spec, vm),
         scratch_shapes=[
             V((2, NM, 2, HALF, 128), BF), V((2, 32, 16384), F32),

time: 78.8 us -> 71.8 us (0.911)
  Pallas kernels: 75.2 us -> 71 us
  local copies, waits for them, and re-layouts: 2.79 us -> 0 us
    pallas_call x1, Pallas kernels: 71.7 us -> 68.1 us  [body(): pl.pallas_call(kernel, out_shape=(V((128, 256), F32), V((2, NM, 2, HALF,...]
    unnamed x6 -> x0, local copies, waits for them, and re-layouts: 2.79 us -> none
where the time goes in v3:
time: 71.8 us; the launch traced here: 71.7 us
  Pallas kernels  71 us (99%)
    pallas_call x1, Pallas kernels, body(): pl.pallas_call(kernel, out_shape=(V((128, 256), F32), V((2, NM, 2, HALF,...  68.1 us
    pallas_call x1, Pallas kernels, body(): pl.pallas_call(expand, out_shape=(jax.ShapeDtypeStruct((2, 32, 16384), F3...  2.95 us

profile of v3, /device:TPU:1, one launch (start us, length us, event | category | flops | bytes accessed | tf_op | source)
XLA Modules:
  0.0 71.7 jit_solution(11008327784410396294)
XLA Ops:
  0.6 68.1 %grads.1 = (f32[128,256]{1,0:T(8,128)S(1)}, bf16[2,64,2,16,128]{4,3,2,1,0:T(8,128)(2,1)S(1)}, f32[2,128,128]{2,1,0:T(8,128)S(1)}) custom-call(bf16[256,128]{1,0:T(8,128)(2,1)} %tok_ref.1, bf16[256,256]{1,0:T(8,128)(2,1)} %g_ref.1, bf16[256,256]{1,0:T(8,128)(2,1)} %u_ref.1, bf16[256,256]{1,0:T(8,128)(2,1)} %h_ref.1, bf16[8192,256]{1,0:T(8,128)(2,1)} %wg_ref.1, ...), custom_call_target="tpu_custom_call" | custom-call | tf_op jit(solution)/shard_map/grads/pallas_call | solution.py:455
  68.7 3.0 %expand.1 = (f32[2,32,16384]{2,1,0:T(8,128)}, bf16[256,128]{1,0:T(8,128)(2,1)}) custom-call(bf16[2,64,2,16,128]{4,3,2,1,0:T(8,128)(2,1)S(1)} %get-tuple-element.7.recv_ref, f32[2,128,128]{2,1,0:T(8,128)S(1)} %get-tuple-element.8.fac_ref, f32[128,256]{1,0:T(8,128)S(1)} %get-tuple-element.9.igt_ref), custom_call_target="tpu_custom_call" | custom-call | tf_op jit(solution)/shard_map/expand/pallas_call | solution.py:487

commit v4 on v2

--- a/solution.py
+++ b/solution.py
@@ -24,18 +24,19 @@
 
 
 SCHEDULE = (
-    ("xt",), ("ga",), ("zs",), ("y", 0), ("ys",), ("gx",), ("mk",), ("il",), ("i", "o"), ("i", "p"),
-    ("y", 1), ("i", "m"), ("i", "s"), ("k", 1), ("bk", 0), ("c", "o"), ("r1",), ("o", 0), ("y", 2),
-    ("b", "s"), ("k", 2), ("bk", 1), ("o", 1), ("c", "p"), ("c", "m"), ("c", "s"), ("o", 2),
-    ("k", 3), ("bk", 2), ("r2",), ("b", "m"), ("b", "p"), ("k", 4), ("bk", 3), ("b", "o"), ("w", 0),
-    ("bk", 4), ("w", 1, 0, 1), ("rz", 4), ("w", 1, 1, 2), ("rz", 3), ("w", 1, 2, 3), ("rz", 2),
-    ("w", 1, 3, 4), ("rz", 1), ("rz", 0),
+    ("xt",), ("ga",), ("gx",), ("mk",), ("il",), ("i", "o"), ("i", "p"), ("i", "m"), ("i", "s"),
+    ("zs",), ("y", 0), ("ys",), ("c", "o"), ("r1",), ("y", 1), ("k", 1), ("bk", 0), ("o", 0),
+    ("y", 2), ("c", "p"), ("c", "m"), ("c", "s"), ("k", 2), ("bk", 1), ("o", 1), ("y", 3),
+    ("b", "s"), ("o", 2), ("k", 3), ("bk", 2), ("o", 3), ("r2",), ("b", "m"), ("b", "p"), ("k", 4),
+    ("bk", 3), ("b", "o"), ("w", 0), ("bk", 4), ("w", 1, 0, 1), ("rz", 4), ("w", 1, 1, 2),
+    ("rz", 3), ("w", 1, 2, 3), ("rz", 2), ("w", 1, 3, 4), ("rz", 1), ("rz", 0),
 )
 
 
 def kernel(
-    tok_ref, g_ref, u_ref, h_ref, wg_ref, wu_ref, mask_ref, perm_ref, exp_ref,
+    tok_ref, g_ref, u_ref, h_ref, wg_ref, wu_ref, mask_hbm, perm_hbm, exp_hbm,
     ig_ref, recv_ref, fac_ref,
+    mask_ref, perm_ref, exp_ref,
     tok, gact, uact, hgrad, wg, wu, xsrc, tt0, tt1, G, GT, wm, facx, lhs, fs, abuf,
     part, crecv, ysum, yrA, yrB, yr2m, yr2p, zra, zrb, zr,
     ss, rs, a_ss, a_rs, lsem,
@@ -64,6 +65,12 @@
         ((tok_ref, tok), (g_ref, gact), (u_ref, uact), (h_ref, hgrad))
     ):
         cp = pltpu.make_async_copy(src, dst, lsem.at[i])
+        cp.start()
+        loads.append(cp)
+    for i, (src, dst) in enumerate(
+        ((mask_hbm, mask_ref), (perm_hbm, perm_ref), (exp_hbm, exp_ref))
+    ):
+        cp = pltpu.make_async_copy(src, dst, lsem.at[8 + i])
         cp.start()
         loads.append(cp)
     wloads = []
@@ -123,7 +130,7 @@
         for d in (1, 7, 2, 6, 3, 5, 4):
             Z[d] = Remote(tt0.at[c, y, 0], tt0.at[c, y, static_slot(-d)], dev_z(d))
 
-    groups = ((0, 1, ()), (1, 3, (1, 7)), (3, 8, (2, 6, 3, 5, 4)))
+    groups = ((0, 1, ()), (1, 3, (1, 7)), (3, 5, (2, 6)), (5, 8, (3, 5, 4)))
 
     def y_first(g):
         s0, s1, ds = groups[g]
@@ -142,15 +149,19 @@
         r = tt0.at[c, yp, pl.ds(s0, s1 - s0), pl.ds(2, 2)]
         O[g, 1] = Remote(r, r, dev_ym)
 
-    def sibling(col):
-        for g in range(3):
+    def sibling(col, g0=0, g1=4):
+        for g in range(g0, g1):
             if col == "o":
                 O[g, 0].recv()
                 O[g, 1].recv()
-            elif col != "s":
+            elif col == "s":
+                for d in groups[g][2]:
+                    Z[d].recv()
+            else:
                 Y[g, col].recv()
-        r = tt0.at[c, cols[col]]
-        S[0, col] = Remote(r, r, dev_sib)
+        s0, s1 = groups[g0][0], groups[g1 - 1][1]
+        r = tt0.at[c, cols[col], pl.ds(s0, s1 - s0)]
+        S[0, (col, g0)] = Remote(r, r, dev_sib)
 
     def y_start():
         for d in (1, 3, 2):
@@ -187,7 +198,7 @@
         S[1, g] = Remote(r, r, dev_sib)
 
     def act_grads():
-        for cp in loads[1:]:
+        for cp in loads[1:4]:
             cp.wait()
         gf = gact[...].astype(F32)
         hf = hgrad[...].astype(F32)
@@ -204,6 +215,8 @@
             X["g", d] = Remote(G.at[q], G.at[q], dev_x(d))
 
     def masks():
+        for cp in loads[4:]:
+            cp.wait()
         lane = lax.broadcasted_iota(jnp.int32, (2, NM, 128), 2)
         for j in range(2):
             pick = lane == 2 * m + j
@@ -216,7 +229,7 @@
             row = perm_ref[w, m]
             mrow = mask_ref[w, pl.ds(row, 1), :].astype(F32)
             erow = exp_ref[w, pl.ds(row, 1), :].astype(F32)
-            fac_ref[w : w + 1, :] = mrow * jnp.exp2(erow)
+            fac_ref[w] = jnp.broadcast_to(mrow * jnp.exp2(erow), (128, 128)).T
 
     def ig_load():
         for cp in wloads:
@@ -375,31 +388,24 @@
         r.copy.wait_send()
 
 
-def expand(recv_ref, fac_ref, igt_ref, out_ref, ig_ref, rbuf, obuf, lsem, osem):
+def expand(recv_ref, fac_ref, igt_ref, out_ref, ig_ref, obuf, osem):
     n = 4
     per = NM // n
-    ins = []
-    for g in range(n):
-        part = pl.ds(g * per, per)
-        cp = pltpu.make_async_copy(recv_ref.at[:, part], rbuf.at[:, part], lsem.at[g])
-        cp.start()
-        ins.append(cp)
-    ig_ref[...] = igt_ref[...].T.astype(BF)
     outs = []
     for g in range(n):
-        ins[g].wait()
         for i in range(g * per, (g + 1) * per):
             for w in range(2):
                 for h in range(2):
-                    v = rbuf[h, i, w].astype(F32)
+                    v = recv_ref[h, i, w].astype(F32)
                     for j in range(2):
                         col = (i * 2 + j) * 128
-                        f = fac_ref[w, i * 2 + j]
+                        f = fac_ref[w, i * 2 + j : i * 2 + j + 1, :]
                         obuf[w, h * HALF : (h + 1) * HALF, col : col + 128] = v * f
         cols = pl.ds(g * per * 256, per * 256)
         cp = pltpu.make_async_copy(obuf.at[:, :, cols], out_ref.at[:, :, cols], osem.at[g])
         cp.start()
         outs.append(cp)
+    ig_ref[...] = igt_ref[...].T.astype(BF)
     for cp in outs:
         cp.wait()
 
@@ -407,18 +413,18 @@
 def body(tokens, gate_act, up_act, hidden_grad, gate_weight, up_weight, block_mask, row_perm, scale_exp):
     any_spec = pl.BlockSpec(memory_space=pl.ANY)
     vm = pl.BlockSpec(memory_space=pltpu.VMEM)
-    sm = pl.BlockSpec(memory_space=pltpu.SMEM)
     V = pltpu.VMEM
     igt, recv, fac = pl.pallas_call(
         kernel,
         out_shape=(
-            jax.ShapeDtypeStruct((128, 256), F32),
-            jax.ShapeDtypeStruct((2, NM, 2, HALF, 128), BF),
-            jax.ShapeDtypeStruct((2, 128), F32),
+            V((128, 256), F32),
+            V((2, NM, 2, HALF, 128), BF),
+            V((2, 128, 128), F32),
         ),
-        in_specs=[any_spec] * 6 + [vm, sm, vm],
+        in_specs=[any_spec] * 9,
         out_specs=(vm, any_spec, vm),
         scratch_shapes=[
+            V((2, NM, 128), jnp.int32), pltpu.SMEM((2, NM), jnp.int32), V((2, NM, 128), jnp.int32),
             V((256, 128), BF), V((256, 256), BF), V((256, 256), BF), V((256, 256), BF),
             V((8192, 256), BF), V((8192, 256), BF),
             V((2, NX, HALF, 256), BF),
@@ -432,7 +438,7 @@
             V((64, 256), BF), V((64, 256), BF), V((2, 3, 128, 256), BF),
             pltpu.SemaphoreType.DMA((N_SEM,)), pltpu.SemaphoreType.DMA((N_SEM,)),
             pltpu.SemaphoreType.DMA((2,)), pltpu.SemaphoreType.DMA((2,)),
-            pltpu.SemaphoreType.DMA((8,)),
+            pltpu.SemaphoreType.DMA((11,)),
         ],
         compiler_params=pltpu.CompilerParams(
             collective_id=0, has_side_effects=True, vmem_limit_bytes=56 << 20
@@ -445,11 +451,10 @@
             jax.ShapeDtypeStruct((2, 32, 16384), F32),
             jax.ShapeDtypeStruct((256, 128), BF),
         ),
-        in_specs=[any_spec, sm, vm],
+        in_specs=[vm, vm, vm],
         out_specs=(any_spec, vm),
         scratch_shapes=[
-            V((2, NM, 2, HALF, 128), BF), V((2, 32, 16384), F32),
-            pltpu.SemaphoreType.DMA((4,)), pltpu.SemaphoreType.DMA((4,)),
+            V((2, 32, 16384), F32), pltpu.SemaphoreType.DMA((4,)),
         ],
         compiler_params=pltpu.CompilerParams(vmem_limit_bytes=32 << 20),
         name="expand",

time: 78.8 us -> 71.2 us (0.904)
  Pallas kernels: 75.2 us -> 70.5 us
  local copies, waits for them, and re-layouts: 2.79 us -> 0 us
    pallas_call x1, Pallas kernels: 71.7 us -> 67.8 us  [body(): pl.pallas_call(kernel, out_shape=(V((128, 256), F32), V((2, NM, 2, HALF,...]
    unnamed x6 -> x0, local copies, waits for them, and re-layouts: 2.79 us -> none
where the time goes in v4:
time: 71.2 us
  Pallas kernels  70.5 us (99%)
    pallas_call x1, Pallas kernels, body(): pl.pallas_call(kernel, out_shape=(V((128, 256), F32), V((2, NM, 2, HALF,...  67.8 us
    pallas_call x1, Pallas kernels, body(): pl.pallas_call(expand, out_shape=(jax.ShapeDtypeStruct((2, 32, 16384), F3...  2.75 us

profile of v4, /device:TPU:1, one launch (start us, length us, event | category | flops | bytes accessed | tf_op | source)
XLA Modules:
  0.0 71.2 jit_solution(455906916049236776)
XLA Ops:
  0.6 67.8 %grads.1 = (f32[128,256]{1,0:T(8,128)S(1)}, bf16[2,64,2,16,128]{4,3,2,1,0:T(8,128)(2,1)S(1)}, f32[2,128,128]{2,1,0:T(8,128)S(1)}) custom-call(bf16[256,128]{1,0:T(8,128)(2,1)} %tok_ref.1, bf16[256,256]{1,0:T(8,128)(2,1)} %g_ref.1, bf16[256,256]{1,0:T(8,128)(2,1)} %u_ref.1, bf16[256,256]{1,0:T(8,128)(2,1)} %h_ref.1, bf16[8192,256]{1,0:T(8,128)(2,1)} %wg_ref.1, ...), custom_call_target="tpu_custom_call" | custom-call | tf_op jit(solution)/shard_map/grads/pallas_call | solution.py:417
  68.4 2.8 %expand.1 = (f32[2,32,16384]{2,1,0:T(8,128)}, bf16[256,128]{1,0:T(8,128)(2,1)}) custom-call(bf16[2,64,2,16,128]{4,3,2,1,0:T(8,128)(2,1)S(1)} %get-tuple-element.7.recv_ref, f32[2,128,128]{2,1,0:T(8,128)S(1)} %get-tuple-element.8.fac_ref, f32[128,256]{1,0:T(8,128)S(1)} %get-tuple-element.9.igt_ref), custom_call_target="tpu_custom_call" | custom-call | tf_op jit(solution)/shard_map/expand/pallas_call | solution.py:448
